TPU v7x, 32 devices: a whole 2x2x4 slice. The times are simulated.
32 devices in a mesh: lat: 8 (over y, x, core), chan: 4 (over z).
Axes of the slice: x: 2, y: 2, z: 4, core: 2. Of those that a mesh axis runs over, the one named last changes fastest.
Arguments:
- grid_field: bfloat16 [8, 2, 384, 1440], P('lat', None, 'chan'), may hold values from -6 to 6
- cotangent: bfloat16 [8, 2, 384, 1440], P('lat', None, 'chan'), may hold values from -6 to 6
- legendre: bfloat16 [40, 1361, 8], P('lat'), may hold values from -1.5 to 1.5
- spectral: float32 [384, 2, 720], P('chan'), may hold values from -3 to 3
- mixing: bfloat16 [384, 384], P(None, 'chan'), may hold values from -0.3125 to 0.3125
- pair_table: int32 [40], replicated, may hold values from 0 to 39, each once
Outputs:
- block_output: bfloat16 [8, 2, 384, 1440], P('lat', None, 'chan')
- grad_input: bfloat16 [8, 2, 384, 1440], P('lat', None, 'chan')
- grad_weights: float32 [384, 2, 720], P('chan')
- grad_mixing: float32 [384, 384], P(None, 'chan')
Inputs may be any that keep to these rules, and one draw needn't show every extreme that they name: `pair_table`: each pair p stands for the orders p and 79 - p, whose degree ranges together fill 1361 coefficients. Index i of lat owns the slots i * 5 to (i + 1) * 5 - 1.
All inputs are finite; a program needn't handle non-finite values.
Results may differ from a plain program's by a relative error of at most 0.0067.
Values may be sent and summed in bfloat16 or wider, within the bound.
A program may use at most 128 MiB of HBM per device.

v0:
```python
import math
import jax
import jax.numpy as jnp
from jax import lax
from jax.sharding import PartitionSpec as P


def dft_basis(orders, longitudes):
    lon_index = jnp.arange(longitudes, dtype=jnp.int32)
    turns = lon_index[:, None] * orders[None, :] % longitudes
    angles = turns.astype(jnp.float32) * (2.0 * math.pi / longitudes)
    norm_scale = 1.0 / math.sqrt(longitudes)
    basis = jnp.stack([jnp.cos(angles) * norm_scale, -jnp.sin(angles) * norm_scale], axis=1)
    return basis.astype(jnp.bfloat16)


def even_odd(spectrum):
    return jnp.stack(
        [spectrum[:, 0] + spectrum[:, 1], spectrum[:, 0] - spectrum[:, 1]], axis=1
    ).astype(jnp.bfloat16)


def local(grid_field, cotangent, legendre, spectral, mixing, pair_table):
    lat_count = lax.axis_size("lat")
    owned = legendre.shape[0]
    packed = legendre.shape[1]
    npairs = legendre.shape[2]
    degrees = spectral.shape[2]
    chan_width = grid_field.shape[2]
    longitudes = grid_field.shape[3]
    order_count = 2 * owned * lat_count
    slot_orders = jnp.stack([pair_table, order_count - 1 - pair_table], axis=1).reshape(-1)
    basis = dft_basis(slot_orders, longitudes)
    weight_m = jnp.where(slot_orders == 0, 1.0, 2.0).astype(jnp.float32)
    spec_x = jnp.einsum("khcj,jrm->khcrm", grid_field, basis, preferred_element_type=jnp.float32)
    spec_g = (
        jnp.einsum("khcj,jrm->khcrm", cotangent, basis, preferred_element_type=jnp.float32)
        * weight_m
    )
    recv_x, recv_g = (
        lax.all_to_all(even_odd(spec_x), "lat", split_axis=4, concat_axis=0, tiled=True),
        lax.all_to_all(even_odd(spec_g), "lat", split_axis=4, concat_axis=0, tiled=True),
    )
    owner_shape = (npairs, 2, chan_width, 2, owned, 2)
    recv_x = recv_x.reshape(owner_shape)
    recv_g = recv_g.reshape(owner_shape)
    slot_start = lax.axis_index("lat") * owned
    lower = lax.dynamic_slice_in_dim(pair_table, slot_start, owned)
    position = jnp.arange(packed, dtype=jnp.int32)[None, :]
    lower_col = lower[:, None]
    leading = position < degrees - lower_col
    degree = jnp.where(leading, lower_col + position, position - (degrees - order_count + 1))
    order = jnp.where(leading, lower_col, order_count - 1 - lower_col)
    half_pick = jnp.where(leading, 0, 1)
    parity = (degree + order) % 2
    two_index = jnp.arange(2, dtype=jnp.int32)
    selector = (
        (half_pick[:, None, None, :] == two_index[None, :, None, None])
        & (parity[:, None, None, :] == two_index[None, None, :, None])
    ).astype(jnp.float32)

    def analyse(received):
        variants = jnp.einsum(
            "pqk,kecrph->phercq", legendre, received, preferred_element_type=jnp.float32
        )
        return jnp.sum(variants * selector[:, :, :, None, None, :], axis=(1, 2))

    coeff_x = analyse(recv_x)
    coeff_g = analyse(recv_g)
    weight_rows = jnp.transpose(spectral, (1, 0, 2))
    weight_pad = jnp.concatenate(
        [weight_rows, jnp.zeros((2, chan_width, packed), jnp.float32)], axis=2
    )
    weight_tail = jnp.concatenate(
        [jnp.zeros((2, chan_width, degrees - order_count + 1), jnp.float32), weight_rows], axis=2
    )
    picked_lead = jnp.stack(
        [lax.dynamic_slice_in_dim(weight_pad, lower[slot], packed, 2) for slot in range(owned)]
    )
    picked = jnp.where(leading[:, None, None, :], picked_lead, weight_tail[None])
    real_w, imag_w = (picked[:, 0], picked[:, 1])
    real_x, imag_x = (coeff_x[:, 0], coeff_x[:, 1])
    real_g, imag_g = (coeff_g[:, 0], coeff_g[:, 1])
    filtered = jnp.stack(
        [real_w * real_x - imag_w * imag_x, real_w * imag_x + imag_w * real_x], axis=1
    ).astype(jnp.bfloat16)
    back_coeff = jnp.stack(
        [real_w * real_g + imag_w * imag_g, real_w * imag_g - imag_w * real_g], axis=1
    ).astype(jnp.bfloat16)
    grad_term = jnp.stack(
        [real_g * real_x + imag_g * imag_x, imag_g * real_x - real_g * imag_x], axis=1
    )
    grad_rows = jnp.zeros((2, chan_width, degrees + packed), jnp.float32)
    for slot in range(owned):
        head_part = jnp.where(leading[slot][None, None, :], grad_term[slot], 0.0)
        current = lax.dynamic_slice_in_dim(grad_rows, lower[slot], packed, 2)
        grad_rows = lax.dynamic_update_slice_in_dim(grad_rows, current + head_part, lower[slot], 2)
    tail_part = jnp.sum(jnp.where(leading[:, None, None, :], 0.0, grad_term), axis=0)
    grad_local = jnp.transpose(
        grad_rows[:, :, :degrees] + tail_part[:, :, degrees - order_count + 1 :], (1, 0, 2)
    )

    def synthesize(coeff):
        masked = (
            coeff[:, None, None].astype(jnp.float32) * selector[:, :, :, None, None, :]
        ).astype(jnp.bfloat16)
        both = jnp.einsum(
            "pqk,phercq->kecrph", legendre, masked, preferred_element_type=jnp.float32
        )
        return even_odd(both.reshape(npairs, 2, chan_width, 2, 2 * owned))

    row_y, row_dx = (
        lax.all_to_all(synthesize(filtered), "lat", split_axis=0, concat_axis=4, tiled=True),
        lax.all_to_all(synthesize(back_coeff), "lat", split_axis=0, concat_axis=4, tiled=True),
    )
    filtered_grid = jnp.einsum(
        "khcrm,jrm->khcj",
        row_y * weight_m.astype(jnp.bfloat16),
        basis,
        preferred_element_type=jnp.float32,
    )
    back_grid = jnp.einsum("khcrm,jrm->khcj", row_dx, basis, preferred_element_type=jnp.float32)
    field_full, cot_full, mixing_full = (
        lax.all_gather(grid_field, "chan", axis=2, tiled=True),
        lax.all_gather(cotangent, "chan", axis=2, tiled=True),
        lax.all_gather(mixing, "chan", axis=1, tiled=True),
    )
    mixing_own = lax.dynamic_slice_in_dim(
        mixing_full, lax.axis_index("chan") * chan_width, chan_width, 0
    )
    skip_path = jnp.einsum("khij,io->khoj", field_full, mixing, preferred_element_type=jnp.float32)
    back_skip = jnp.einsum(
        "khoj,io->khij", cot_full, mixing_own, preferred_element_type=jnp.float32
    )
    mixing_grad = jnp.einsum(
        "khij,khoj->io", field_full, cotangent, preferred_element_type=jnp.float32
    )
    block_output = (filtered_grid + skip_path).astype(jnp.bfloat16)
    grad_input = (back_grid + back_skip).astype(jnp.bfloat16)
    weight_sum, mixing_sum = lax.psum((grad_local, mixing_grad), "lat")
    grad_weights = weight_sum / math.sqrt(order_count)
    grad_mixing = mixing_sum / math.sqrt(2 * npairs * longitudes)
    return (block_output, grad_input, grad_weights, grad_mixing)


def solution(mesh):
    in_specs = (
        P("lat", None, "chan", None),
        P("lat", None, "chan", None),
        P("lat", None, None),
        P("chan", None, None),
        P(None, "chan"),
        P(),
    )
    out_specs = (
        P("lat", None, "chan", None),
        P("lat", None, "chan", None),
        P("chan", None, None),
        P(None, "chan"),
    )
    return jax.shard_map(local, mesh=mesh, in_specs=in_specs, out_specs=out_specs, check_vma=False)
```

profile of v0, /device:TPU:0, one launch (start us, length us, event | category | flops | bytes accessed | tf_op | source)
XLA Modules:
  0.0 241.8 jit_solution(9440944002188104553)
XLA Ops:
  16.6 5.2 %all-to-all-start.2 = ((bf16[1,2,96,2,80]{2,1,3,0,4:T(2,128)(2,1)}), bf16[1,2,96,2,80]{2,1,3,0,4:T(2,128)(2,1)S(1)}, u32[]{:S(2)}, u32[]{:S(2)}) async-start(bf16[1,2,96,2,80]{2,1,3,0,4:T(2,128)(2,1)} %copy.58), calls=%async_computation.2 | async-start | bytes 163840 | tf_op jit(solution)/shard_map/all_to_all | solution.py:42
  34.2 3.9 %pad_dynamic-slice_fusion = (f32[2,96,1361]{2,0,1:T(2,128)S(1)}, f32[2,96,1361]{2,0,1:T(2,128)S(1)}, f32[2,96,1361]{2,0,1:T(2,128)S(1)}, f32[2,96,1361]{2,0,1:T(2,128)S(1)}, f32[2,96,1361]{2,0,1:T(2,128)S(1)}) fusion(s32[]{:T(128)S(6)} %select_n.122, f32[2,96,720]{2,0,1:T(2,128)S(1)} %bitcast.169, s32[]{:T(128)S(6)} %select_n.119, s32[]{:T(128)S(6)} %select_n.120, ...), kind=kLoop, calls=%fused_computation.40 | loop fusion | bytes 5779220 | tf_op jit(solution)/shard_map/dynamic_slice | solution.py:78
  38.9 2.8 %broadcast_select_fusion = f32[5,2,96,1361]{3,2,1,0:T(8,128)} fusion(f32[5,2,96,1361]{3,2,1,0:T(8,128)S(1)} %bitcast_dynamic-update-slice_fusion, f32[2,96,1361]{2,1,0:T(8,128)S(1)} %concatenate.35.clone, pred[5,1361]{1,0:T(8,128)(4,1)S(1)} %iota_compare_fusion.2), kind=kLoop, calls=%fused_computation.31 | loop fusion | flops 1306560 | bytes 11504533 | tf_op jit(solution)/shard_map/jit(_where)/select_n | solution.py:80
  41.9 17.9 %all_gather.10 = bf16[384,384]{0,1:T(8,128)(2,1)} all-gather(bf16[384,96]{0,1:T(8,128)(2,1)S(1)} %copy-done.17), channel_id=1, replica_groups=mesh['lat'=8,'chan'=4] {'chan'}, dimensions={1}, use_global_device_ids=true | all-gather | bytes 368640 | tf_op jit(solution)/shard_map/all_gather | solution.py:126
  60.6 4.1 %all-to-all-start = ((bf16[1,2,96,2,80]{2,1,3,0,4:T(2,128)(2,1)}), bf16[1,2,96,2,80]{2,1,3,0,4:T(2,128)(2,1)S(1)}, u32[]{:S(2)}, u32[]{:S(2)}) async-start(bf16[1,2,96,2,80]{2,1,3,0,4:T(2,128)(2,1)} %copy.47), calls=%async_computation | async-start | bytes 163840 | tf_op jit(solution)/shard_map/all_to_all | solution.py:41
  64.7 6.0 %fusion = f32[5,2,96,1361]{3,2,1,0:T(8,128)} fusion(f32[5,2,2,1361]{3,1,2,0:T(2,128)S(1)} %and_convert_fusion, bf16[5,1361,8]{1,2,0:T(8,128)(2,1)S(1)} %copy-done, bf16[8,2,96,2,5,2]{2,1,3,5,4,0:T(2,128)(2,1)S(1)} %bitcast.176), kind=kOutput, calls=%fused_computation.1 | convolution fusion | flops 92765760 | bytes 5505440 | tf_op jit(solution)/shard_map/pqk,kecrph->phercq/dot_general | solution.py:63
  70.7 3.7 %fusion.1 = f32[5,2,96,1361]{3,2,1,0:T(8,128)S(1)} fusion(f32[5,2,2,1361]{3,1,2,0:T(2,128)S(1)} %and_convert_fusion, bf16[5,1361,8]{1,2,0:T(8,128)(2,1)S(1)} %copy-done, bf16[8,2,96,2,5,2]{2,1,3,5,4,0:T(2,128)(2,1)S(1)} %bitcast.177), kind=kOutput, calls=%fused_computation.3 | convolution fusion | flops 92765760 | bytes 5505440 | tf_op jit(solution)/shard_map/pqk,kecrph->phercq/dot_general | solution.py:63
  74.4 5.7 %add_convert_fusion = (bf16[5,1,96,1361]{3,2,1,0:T(8,128)(2,1)}, bf16[5,1,96,1361]{3,2,1,0:T(8,128)(2,1)}) fusion(f32[5,2,96,1361]{3,2,1,0:T(8,128)S(1)} %copy-done.6, f32[5,2,96,1361]{3,2,1,0:T(8,128)} %broadcast_select_fusion), kind=kLoop, calls=%fused_computation.28 | loop fusion | flops 5226240 | bytes 13065600 | tf_op jit(solution)/shard_map/convert.2
  85.9 6.5 %dynamic_update_slice.15 = f32[2,96,2081]{2,1,0:T(8,128)} dynamic-update-slice(f32[2,96,2081]{2,1,0:T(8,128)} %broadcast_in_dim.141, f32[2,96,1361]{2,1,0:T(8,128)} %fusion.22, s32[]{:T(128)} %constant.26.clone.1, s32[]{:T(128)} %constant.26.clone.1, s32[]{:T(128)S(6)} %select_n.118) | dynamic-update-slice | bytes 2090500 | tf_op jit(solution)/shard_map/dynamic_update_slice | solution.py:97
  92.4 2.8 %fusion.26 = f32[2,96,1361]{2,1,0:T(8,128)} fusion(f32[5,1,96,1361]{3,2,1,0:T(8,128)S(1)} %get-tuple-element.17, f32[5,1,96,1361]{3,2,1,0:T(8,128)} %copy-done.1, f32[2,96,2081]{2,1,0:T(8,128)} %dynamic_update_slice.15, s32[]{:T(128)S(6)} %select_n.119, pred[1361]{0:T(1024)(128)(4,1)S(1)} %get-tuple-element.10), kind=kLoop, calls=%fused_computation.59 | loop fusion | flops 783936 | bytes 7318101 | tf_op jit(solution)/shard_map/add | solution.py:97
  95.2 6.5 %dynamic_update_slice.16 = f32[2,96,2081]{2,1,0:T(8,128)} dynamic-update-slice(f32[2,96,2081]{2,1,0:T(8,128)} %dynamic_update_slice.15, f32[2,96,1361]{2,1,0:T(8,128)} %fusion.26, s32[]{:T(128)} %constant.26.clone.1, s32[]{:T(128)} %constant.26.clone.1, s32[]{:T(128)S(6)} %select_n.119) | dynamic-update-slice | bytes 2090500 | tf_op jit(solution)/shard_map/dynamic_update_slice | solution.py:97
  101.7 2.8 %fusion.30 = f32[2,96,1361]{2,1,0:T(8,128)} fusion(f32[5,1,96,1361]{3,2,1,0:T(8,128)S(1)} %get-tuple-element.17, f32[5,1,96,1361]{3,2,1,0:T(8,128)} %copy-done.1, f32[2,96,2081]{2,1,0:T(8,128)} %dynamic_update_slice.16, s32[]{:T(128)S(6)} %select_n.120, pred[1361]{0:T(1024)(128)(4,1)S(1)} %get-tuple-element.9), kind=kLoop, calls=%fused_computation.63 | loop fusion | flops 783936 | bytes 7318101 | tf_op jit(solution)/shard_map/add | solution.py:97
  104.5 6.5 %dynamic_update_slice.17 = f32[2,96,2081]{2,1,0:T(8,128)} dynamic-update-slice(f32[2,96,2081]{2,1,0:T(8,128)} %dynamic_update_slice.16, f32[2,96,1361]{2,1,0:T(8,128)} %fusion.30, s32[]{:T(128)} %constant.26.clone.1, s32[]{:T(128)} %constant.26.clone.1, s32[]{:T(128)S(6)} %select_n.120) | dynamic-update-slice | bytes 2090500 | tf_op jit(solution)/shard_map/dynamic_update_slice | solution.py:97
  113.9 9.1 %multiply_convert_fusion = (bf16[5,2,2,2,96,1361]{5,4,1,3,2,0:T(8,128)(2,1)}, bf16[5,2,2,2,96,1361]{5,4,1,3,2,0:T(8,128)(2,1)}) fusion(f32[5,2,96,1361]{3,2,1,0:T(8,128)S(1)} %maximum_convert_fusion.1, f32[5,2,2,1361]{3,1,2,0:T(2,128)S(1)} %and_convert_fusion, f32[5,2,96,1361]{3,2,1,0:T(8,128)S(1)} %maximum_convert_fusion), kind=kLoop, calls=%fused_computation.4 | loop fusion | flops 20904960 | bytes 31466320 | tf_op jit(solution)/shard_map/convert_element_type | solution.py:106
  122.9 6.4 %fusion.2 = f32[5,2,2,2,96,8]{4,5,3,2,1,0:T(8,128)S(1)} fusion(bf16[5,2,2,2,96,1361]{5,4,1,3,2,0:T(8,128)(2,1)} %get-tuple-element.42, bf16[5,1361,8]{1,2,0:T(8,128)(2,1)S(1)} %copy-done), kind=kOutput, calls=%fused_computation.6 | convolution fusion | flops 83619840 | bytes 10684240 | tf_op jit(solution)/shard_map/pqk,phercq->kecrph/dot_general | solution.py:107
  131.4 6.5 %dynamic_update_slice.18 = f32[2,96,2081]{2,1,0:T(8,128)} dynamic-update-slice(f32[2,96,2081]{2,1,0:T(8,128)} %dynamic_update_slice.17, f32[2,96,1361]{2,1,0:T(8,128)} %fusion.34, s32[]{:T(128)} %constant.26.clone.1, s32[]{:T(128)} %constant.26.clone.1, s32[]{:T(128)S(6)} %select_n.121) | dynamic-update-slice | bytes 2090500 | tf_op jit(solution)/shard_map/dynamic_update_slice | solution.py:97
  139.6 4.2 %all-to-all-start.3 = ((bf16[8,2,96,2,10]{2,3,4,1,0:T(2,128)(2,1)}), bf16[8,2,96,2,10]{2,3,4,1,0:T(2,128)(2,1)S(1)}, u32[]{:S(2)}, u32[]{:S(2)}) async-start(bf16[8,2,96,2,10]{2,3,4,1,0:T(2,128)(2,1)} %pad_maximum_fusion.5), calls=%async_computation.3 | async-start | bytes 163840 | tf_op jit(solution)/shard_map/all_to_all | solution.py:114
  143.7 6.4 %fusion.4 = f32[5,2,2,2,96,8]{4,5,3,2,1,0:T(8,128)S(1)} fusion(bf16[5,2,2,2,96,1361]{5,4,1,3,2,0:T(8,128)(2,1)} %get-tuple-element.43, bf16[5,1361,8]{1,2,0:T(8,128)(2,1)S(1)} %copy-done), kind=kOutput, calls=%fused_computation.8 | convolution fusion | flops 83619840 | bytes 10684240 | tf_op jit(solution)/shard_map/pqk,phercq->kecrph/dot_general | solution.py:107
  154.0 6.5 %dynamic_update_slice.19 = f32[2,96,2081]{2,1,0:T(8,128)} dynamic-update-slice(f32[2,96,2081]{2,1,0:T(8,128)} %dynamic_update_slice.18, f32[2,96,1361]{2,1,0:T(8,128)} %fusion.38, s32[]{:T(128)} %constant.26.clone.1, s32[]{:T(128)} %constant.26.clone.1, s32[]{:T(128)S(6)} %select_n.122) | dynamic-update-slice | bytes 2090500 | tf_op jit(solution)/shard_map/dynamic_update_slice | solution.py:97
  160.5 4.2 %all-to-all-start.1 = ((bf16[8,2,96,2,10]{2,3,4,1,0:T(2,128)(2,1)}), bf16[8,2,96,2,10]{2,3,4,1,0:T(2,128)(2,1)S(1)}, u32[]{:S(2)}, u32[]{:S(2)}) async-start(bf16[8,2,96,2,10]{2,3,4,1,0:T(2,128)(2,1)} %pad_maximum_fusion.3), calls=%async_computation.1 | async-start | bytes 163840 | tf_op jit(solution)/shard_map/all_to_all | solution.py:113
  166.9 2.9 %all-to-all-done.1 = bf16[8,2,96,2,10]{2,3,4,1,0:T(2,128)(2,1)S(1)} async-done(((bf16[8,2,96,2,10]{2,3,4,1,0:T(2,128)(2,1)}), bf16[8,2,96,2,10]{2,3,4,1,0:T(2,128)(2,1)S(1)}, u32[]{:S(2)}, u32[]{:S(2)}) %all-to-all-start.1) | async-done | bytes 61472 | tf_op jit(solution)/shard_map/all_to_all | solution.py:113
  170.0 6.1 %copy.57 = bf16[1,2,384,1440]{2,3,1,0:T(8,128)(2,1)S(1)} copy(bf16[1,2,384,1440]{3,1,0,2:T(2,128)(2,1)} %all-gather.3.cloned.1.call-done) | data formatting | bytes 4423680 | tf_op jit(solution)/shard_map/all_gather | solution.py:124
  177.4 6.9 %copy.69 = bf16[1,2,384,1440]{2,3,1,0:T(8,128)(2,1)} copy(bf16[1,2,384,1440]{3,1,0,2:T(2,128)(2,1)} %all-gather.5.cloned.1.call-done) | data formatting | bytes 4423680 | tf_op jit(solution)/shard_map/all_gather | solution.py:125
  190.1 41.2 %all-reduce.5.cloned.1.call-done = (f32[96,2,720]{2,0,1:T(8,128)}, f32[384,96]{0,1:T(8,128)}) async-done(((f32[96,2,720]{2,0,1:T(8,128)}, f32[384,96]{0,1:T(8,128)}), (f32[96,2,720]{2,0,1:T(8,128)}, f32[384,96]{0,1:T(8,128)})) %all-reduce.5.cloned.1.call-update) | async-done | bytes 700432 | tf_op jit(solution)/shard_map/psum | solution.py:140
  (116 shorter events, 43.5 us)
Async XLA Ops:
  7.2 57.5 %copy-start = (bf16[5,1361,8]{1,2,0:T(8,128)(2,1)S(1)}, bf16[5,1361,8]{1,2,0:T(8,128)(2,1)}, u32[]{:S(2)}) copy-start(bf16[5,1361,8]{1,2,0:T(8,128)(2,1)} %param.8) | copy-start | bytes 326644
  7.2 14.7 %copy-start.11 = (bf16[1,2,96,1440]{3,2,1,0:T(8,128)(2,1)S(1)}, bf16[1,2,96,1440]{3,2,1,0:T(8,128)(2,1)}, u32[]{:S(2)}) copy-start(bf16[1,2,96,1440]{3,2,1,0:T(8,128)(2,1)} %param.7) | copy-start | bytes 1658884
  7.2 162.8 %all-gather.3.cloned.1.call-start = ((), (), s32[]{:S(2)}) async-start(), calls=%async_computation.4 | async-start | bytes 2949120 | tf_op jit(solution)/shard_map/all_gather | solution.py:124
  9.8 13.5 %copy-start.19 = (s32[40]{0:T(128)S(1)}, s32[40]{0:T(128)}, u32[]{:S(2)}) copy-start(s32[40]{0:T(128)} %param.11) | copy-start | bytes 484
  9.8 20.7 %copy-start.16 = (bf16[1,2,96,1440]{3,2,1,0:T(8,128)(2,1)S(1)}, bf16[1,2,96,1440]{3,2,1,0:T(8,128)(2,1)}, u32[]{:S(2)}) copy-start(bf16[1,2,96,1440]{3,2,1,0:T(8,128)(2,1)} %param.6) | copy-start | bytes 1658884
  14.2 16.7 %copy-start.12 = (bf16[1440,1,80]{0,2,1:T(8,128)(2,1)}, bf16[1440,1,80]{0,2,1:T(8,128)(2,1)S(1)}, u32[]{:S(2)}) copy-start(bf16[1440,1,80]{0,2,1:T(8,128)(2,1)S(1)} %get-tuple-element.51) | copy-start | bytes 691204
  14.2 16.7 %copy-start.14 = (bf16[1440,1,80]{0,2,1:T(8,128)(2,1)}, bf16[1440,1,80]{0,2,1:T(8,128)(2,1)S(1)}, u32[]{:S(2)}) copy-start(bf16[1440,1,80]{0,2,1:T(8,128)(2,1)S(1)} %get-tuple-element.52) | copy-start | bytes 691204
  14.2 16.7 %copy-start.10 = (f32[96,2,720]{2,1,0:T(2,128)S(1)}, f32[96,2,720]{2,1,0:T(2,128)}, u32[]{:S(2)}) copy-start(f32[96,2,720]{2,1,0:T(2,128)} %param.9) | copy-start | bytes 1658884
  16.6 44.0 %all-to-all-start.2 = ((bf16[1,2,96,2,80]{2,1,3,0,4:T(2,128)(2,1)}), bf16[1,2,96,2,80]{2,1,3,0,4:T(2,128)(2,1)S(1)}, u32[]{:S(2)}, u32[]{:S(2)}) async-start(bf16[1,2,96,2,80]{2,1,3,0,4:T(2,128)(2,1)} %copy.58), calls=%async_computation.2 | async-start | bytes 163840 | tf_op jit(solution)/shard_map/all_to_all | solution.py:42
  21.8 155.6 %all-gather.5.cloned.1.call-start = ((), (), s32[]{:S(2)}) async-start(), calls=%async_computation.5 | async-start | bytes 2949120 | tf_op jit(solution)/shard_map/all_gather | solution.py:125
  38.9 3.1 %copy-start.17 = (bf16[384,96]{0,1:T(8,128)(2,1)S(1)}, bf16[384,96]{0,1:T(8,128)(2,1)}, u32[]{:S(2)}) copy-start(bf16[384,96]{0,1:T(8,128)(2,1)} %param.10) | copy-start | bytes 221188
  60.6 10.1 %all-to-all-start = ((bf16[1,2,96,2,80]{2,1,3,0,4:T(2,128)(2,1)}), bf16[1,2,96,2,80]{2,1,3,0,4:T(2,128)(2,1)S(1)}, u32[]{:S(2)}, u32[]{:S(2)}) async-start(bf16[1,2,96,2,80]{2,1,3,0,4:T(2,128)(2,1)} %copy.47), calls=%async_computation | async-start | bytes 163840 | tf_op jit(solution)/shard_map/all_to_all | solution.py:41
  70.7 3.7 %copy-start.6 = (f32[5,2,96,1361]{3,2,1,0:T(8,128)S(1)}, f32[5,2,96,1361]{3,2,1,0:T(8,128)}, u32[]{:S(2)}) copy-start(f32[5,2,96,1361]{3,2,1,0:T(8,128)} %fusion) | copy-start | bytes 15678724
  70.7 9.4 %slice-start = ((s8[5406720]{0:T(1024)(128)(4,1)}), s8[1212416]{0:T(1024)(128)(4,1)S(1)}, s32[]{:S(2)}) async-start(s8[5406720]{0:T(1024)(128)(4,1)} %bitcast.166), calls=%async_computation.7 | async-start | bytes 2424832
  74.4 5.7 %slice-start.1 = ((s8[5406720]{0:T(1024)(128)(4,1)}), s8[4194304]{0:T(1024)(128)(4,1)S(1)}, s32[]{:S(2)}) async-start(s8[5406720]{0:T(1024)(128)(4,1)} %bitcast.166), calls=%async_computation.8 | async-start | bytes 8388608
  122.9 6.4 %copy-start.2 = (f32[5,1,96,1361]{3,2,1,0:T(8,128)S(1)}, f32[5,1,96,1361]{3,2,1,0:T(8,128)}, u32[]{:S(2)}) copy-start(f32[5,1,96,1361]{3,2,1,0:T(8,128)} %copy-done.1) | copy-start | bytes 7839364
  122.9 6.4 %copy-start.4 = (f32[2,96,2081]{2,1,0:T(8,128)S(1)}, f32[2,96,2081]{2,1,0:T(8,128)}, u32[]{:S(2)}) copy-start(f32[2,96,2081]{2,1,0:T(8,128)} %dynamic_update_slice.17) | copy-start | bytes 4794628
  139.6 20.9 %all-to-all-start.3 = ((bf16[8,2,96,2,10]{2,3,4,1,0:T(2,128)(2,1)}), bf16[8,2,96,2,10]{2,3,4,1,0:T(2,128)(2,1)S(1)}, u32[]{:S(2)}, u32[]{:S(2)}) async-start(bf16[8,2,96,2,10]{2,3,4,1,0:T(2,128)(2,1)} %pad_maximum_fusion.5), calls=%async_computation.3 | async-start | bytes 163840 | tf_op jit(solution)/shard_map/all_to_all | solution.py:114
  143.7 6.6 %copy-start.3 = (f32[5,1,96,1361]{3,2,1,0:T(8,128)S(1)}, f32[5,1,96,1361]{3,2,1,0:T(8,128)}, u32[]{:S(2)}) copy-start(f32[5,1,96,1361]{3,2,1,0:T(8,128)} %copy-done.1) | copy-start | bytes 7839364
  153.2 11.5 %copy-start.9 = (f32[2,96,1361]{2,1,0:T(8,128)S(1)}, f32[2,96,1361]{2,1,0:T(8,128)}, u32[]{:S(2)}) copy-start(f32[2,96,1361]{2,1,0:T(8,128)} %fusion.7) | copy-start | bytes 3135748
  153.2 16.6 %copy-start.20 = (bf16[80]{0:T(256)(128)(2,1)S(1)}, bf16[80]{0:T(256)(128)(2,1)}, u32[]{:S(2)}) copy-start(bf16[80]{0:T(256)(128)(2,1)} %get-tuple-element.45) | copy-start | bytes 484
  160.5 9.3 %all-to-all-start.1 = ((bf16[8,2,96,2,10]{2,3,4,1,0:T(2,128)(2,1)}), bf16[8,2,96,2,10]{2,3,4,1,0:T(2,128)(2,1)S(1)}, u32[]{:S(2)}, u32[]{:S(2)}) async-start(bf16[8,2,96,2,10]{2,3,4,1,0:T(2,128)(2,1)} %pad_maximum_fusion.3), calls=%async_computation.1 | async-start | bytes 163840 | tf_op jit(solution)/shard_map/all_to_all | solution.py:113
  164.6 66.7 %all-reduce.5.cloned.1.call-start = ((), (), s32[]{:S(2)}) async-start(), calls=%async_computation.6 | async-start | bytes 1474560 | tf_op jit(solution)/shard_map/psum | solution.py:140
  184.3 3.9 %copy-start.18 = (bf16[384,96]{0,1:T(8,128)(2,1)S(1)}, bf16[384,96]{0,1:T(8,128)(2,1)}, u32[]{:S(2)}) copy-start(bf16[384,96]{0,1:T(8,128)(2,1)} %param.10) | copy-start | bytes 221188
  (6 other events, 13.6 us)
Sparse Core Ops, SparseCore 0:
  10.2 57.7 all-gather.2
  70.1 49.2 all-gather.4
  177.5 53.8 all-reduce.4
where the time goes:
time: 244 us; the launch traced here: 242 us
  local copies, waits for them, and re-layouts  60.8 us (25%)
  other arithmetic  45.8 us (19%)
  waiting for transfers between devices  44.2 us (18%)
  matrix products  31.6 us (13%)
  between operations  23.8 us (10%)
  blocking collectives  17.9 us (7%)
  starting transfers between devices  17.7 us (7%)
    psum x1, waiting for transfers between devices, local(): weight_sum, mixing_sum = lax.psum((grad_local, mixing_grad), 'lat')  41.2 us
    dynamic_update_slice x5, local copies, waits for them, and re-layouts, local(): lax.dynamic_update_slice_in_dim(grad_rows, current + head_part, lower[slo...  32.4 us
    all_gather x1, blocking collectives, local(): lax.all_gather(mixing, 'chan', axis=1, tiled=True)  17.9 us
    dot_general x2, matrix products, synthesize(): jnp.einsum('pqk,phercq->kecrph', legendre, masked, preferred_element_type...  12.9 us
    dot_general x2, matrix products, analyse(): jnp.einsum('pqk,kecrph->phercq', legendre, received, preferred_element_ty...  9.7 us
    convert_element_type x1, other arithmetic, synthesize(): masked = (coeff[:, None, None].astype(jnp.float32) * selector[:, :, :, No...  9.06 us
    another operation x6, other arithmetic  9 us
    add x4, other arithmetic, local(): current + head_part  8.28 us
  transfers between devices with their start and end apart: 7, of which 2 were waited for; matrix products, arithmetic and copies ran while one was open for 54% of the time, Pallas kernels for 0%

commit v1 on v0

--- a/solution.py
+++ b/solution.py
@@ -3,6 +3,28 @@
 import jax.numpy as jnp
 from jax import lax
 from jax.sharding import PartitionSpec as P
+
+
+def in_blocks(shard, dim, count):
+    before, after = (shard.shape[:dim], shard.shape[dim + 1 :])
+    return jnp.moveaxis(shard.reshape(*before, count, -1, *after), dim, 0)
+
+
+def in_order(pieces, dim):
+    pieces = jnp.moveaxis(pieces, 0, dim)
+    shape = pieces.shape
+    return pieces.reshape(*shape[:dim], shape[dim] * shape[dim + 1], *shape[dim + 2 :])
+
+
+def pairwise_exchange(shard, axis, split_dim, concat_dim):
+    length, here = (lax.axis_size(axis), lax.axis_index(axis))
+    blocks = in_blocks(shard, split_dim, length)
+    finished = [blocks[here]]
+    for step in range(1, length):
+        sent = blocks[here ^ step]
+        finished.append(lax.ppermute(sent, axis, [(i, i ^ step) for i in range(length)]))
+    blocks = jnp.stack(finished)[here ^ jnp.arange(length)]
+    return in_order(blocks, concat_dim)
 
 
 def dft_basis(orders, longitudes):
@@ -39,7 +61,7 @@
     )
     recv_x, recv_g = (
         lax.all_to_all(even_odd(spec_x), "lat", split_axis=4, concat_axis=0, tiled=True),
-        lax.all_to_all(even_odd(spec_g), "lat", split_axis=4, concat_axis=0, tiled=True),
+        pairwise_exchange(even_odd(spec_g), "lat", 4, 0),
     )
     owner_shape = (npairs, 2, chan_width, 2, owned, 2)
     recv_x = recv_x.reshape(owner_shape)

time: 244 us -> 258 us (1.057)
  local copies, waits for them, and re-layouts: 60.8 us -> 73.3 us
  other arithmetic: 45.8 us -> 48.9 us
    unnamed x54 -> x56, local copies, waits for them, and re-layouts: 6.75 us -> 17.8 us
    ppermute x0 -> x7, starting transfers between devices: none -> 7.27 us  [pairwise_exchange(): lax.ppermute(sent, axis, [(i, i ^ step) for i in range(length)])]
    another operation x6, other arithmetic: 9 us -> 3.5 us
    all_to_all x1 -> x0, starting transfers between devices: 5.17 us -> none  [local(): lax.all_to_all(even_odd(spec_g), 'lat', split_axis=4, concat_axis=0, tile...]
    select_n x1, other arithmetic: 2.78 us -> 5.42 us  [local(): jnp.where(leading[:, None, None, :], picked_lead, weight_tail[None])]
  transfers between devices with their start and end apart: 7 -> 13, of which waited for: 2 -> 3; matrix products, arithmetic and copies ran while one was open for 54% -> 56% of each run, Pallas kernels for 0% -> 0%
where the time goes in v1:
time: 258 us; the launch traced here: 255 us
  local copies, waits for them, and re-layouts  73.3 us (28%)
  other arithmetic  48.9 us (19%)
  waiting for transfers between devices  44.8 us (17%)
  matrix products  29.2 us (11%)
  between operations  24.1 us (9%)
  starting transfers between devices  18.8 us (7%)
  blocking collectives  16.3 us (6%)
    psum x1, waiting for transfers between devices, local(): weight_sum, mixing_sum = lax.psum((grad_local, mixing_grad), 'lat')  40.8 us
    dynamic_update_slice x5, local copies, waits for them, and re-layouts, local(): lax.dynamic_update_slice_in_dim(grad_rows, current + head_part, lower[slo...  32.5 us
    unnamed x56, local copies, waits for them, and re-layouts  17.8 us
    all_gather x1, blocking collectives, local(): lax.all_gather(mixing, 'chan', axis=1, tiled=True)  16.3 us
    dot_general x2, matrix products, synthesize(): jnp.einsum('pqk,phercq->kecrph', legendre, masked, preferred_element_type...  12.9 us
    convert_element_type x1, other arithmetic, synthesize(): masked = (coeff[:, None, None].astype(jnp.float32) * selector[:, :, :, No...  10.7 us
    add x4, other arithmetic, local(): current + head_part  8.23 us
    dot_general x2, matrix products, analyse(): jnp.einsum('pqk,kecrph->phercq', legendre, received, preferred_element_ty...  7.36 us
  transfers between devices with their start and end apart: 13, of which 3 were waited for; matrix products, arithmetic and copies ran while one was open for 56% of the time, Pallas kernels for 0%

profile of v1, /device:TPU:0, one launch (start us, length us, event | category | flops | bytes accessed | tf_op | source)
XLA Modules:
  0.0 255.4 jit_solution(2060392895815714533)
XLA Ops:
  22.2 3.9 %all-to-all-start = ((bf16[1,2,96,2,80]{2,1,3,0,4:T(2,128)(2,1)}), bf16[1,2,96,2,80]{2,1,3,0,4:T(2,128)(2,1)S(1)}, u32[]{:S(2)}, u32[]{:S(2)}) async-start(bf16[1,2,96,2,80]{2,1,3,0,4:T(2,128)(2,1)} %copy.68), calls=%async_computation | async-start | bytes 163840 | tf_op jit(solution)/shard_map/all_to_all | solution.py:63
  39.1 4.9 %pad_dynamic-slice_fusion = (f32[2,96,1361]{2,0,1:T(2,128)S(1)}, f32[2,96,1361]{2,0,1:T(2,128)}, f32[2,96,1361]{2,0,1:T(2,128)}, f32[2,96,1361]{2,0,1:T(2,128)S(1)}, f32[2,96,1361]{2,0,1:T(2,128)S(1)}) fusion(s32[]{:T(128)S(6)} %select_n.156, f32[2,96,720]{2,0,1:T(2,128)S(1)} %bitcast.203, s32[]{:T(128)S(6)} %select_n.153, s32[]{:T(128)S(6)} %select_n.154, ...), kind=kLoop, calls=%fused_computation.41 | loop fusion | bytes 5779220 | tf_op jit(solution)/shard_map/dynamic_slice | solution.py:100
  51.1 5.4 %broadcast_select_fusion = f32[5,2,96,1361]{3,2,1,0:T(8,128)} fusion(f32[5,2,96,1361]{3,2,1,0:T(8,128)} %bitcast_dynamic-update-slice_fusion, f32[2,96,1361]{2,1,0:T(8,128)S(1)} %concatenate.36.clone, pred[5,1361]{1,0:T(8,128)(4,1)S(1)} %iota_compare_fusion.2), kind=kLoop, calls=%fused_computation.32 | loop fusion | flops 1306560 | bytes 11504533 | tf_op jit(solution)/shard_map/jit(_where)/select_n | solution.py:102
  56.8 16.3 %all_gather.10 = bf16[384,384]{0,1:T(8,128)(2,1)} all-gather(bf16[384,96]{0,1:T(8,128)(2,1)S(1)} %copy-done.17), channel_id=1, replica_groups=mesh['lat'=8,'chan'=4] {'chan'}, dimensions={1}, use_global_device_ids=true | all-gather | bytes 368640 | tf_op jit(solution)/shard_map/all_gather | solution.py:148
  81.0 3.7 %fusion = f32[5,2,96,1361]{3,2,1,0:T(8,128)S(1)} fusion(f32[5,2,2,1361]{3,1,2,0:T(2,128)S(1)} %and_convert_fusion, bf16[5,1361,8]{1,2,0:T(8,128)(2,1)S(1)} %copy-done, bf16[8,2,96,2,5,2]{2,3,5,4,1,0:T(2,128)(2,1)S(1)} %bitcast.201), kind=kOutput, calls=%fused_computation.2 | convolution fusion | flops 92765760 | bytes 5505440 | tf_op jit(solution)/shard_map/pqk,kecrph->phercq/dot_general | solution.py:85
  87.2 2.8 %maximum_convert_fusion.1 = f32[5,2,96,1361]{3,2,1,0:T(8,128)} fusion(bf16[5,1,96,1361]{3,2,1,0:T(8,128)(2,1)S(1)} %get-tuple-element.20, bf16[5,1,96,1361]{3,2,1,0:T(8,128)(2,1)S(1)} %get-tuple-element.19), kind=kLoop, calls=%fused_computation.25 | loop fusion | flops 2613120 | bytes 7839360 | tf_op jit(solution)/shard_map/convert_element_type | solution.py:127
  90.0 3.7 %fusion.1 = f32[5,2,96,1361]{3,2,1,0:T(8,128)S(1)} fusion(f32[5,2,2,1361]{3,1,2,0:T(2,128)S(1)} %and_convert_fusion, bf16[5,1361,8]{1,2,0:T(8,128)(2,1)S(1)} %copy-done, bf16[8,2,96,2,5,2]{2,1,3,5,4,0:T(2,128)(2,1)S(1)} %bitcast.214), kind=kOutput, calls=%fused_computation.4 | convolution fusion | flops 92765760 | bytes 5505440 | tf_op jit(solution)/shard_map/pqk,kecrph->phercq/dot_general | solution.py:85
  93.7 4.5 %multiply_add_fusion = (f32[5,1,96,1361]{3,2,1,0:T(8,128)S(1)}, f32[5,1,96,1361]{3,2,1,0:T(8,128)S(1)}, bf16[5,1,96,1361]{3,2,1,0:T(8,128)(2,1)}, bf16[5,1,96,1361]{3,2,1,0:T(8,128)(2,1)}) fusion(f32[5,2,96,1361]{3,2,1,0:T(8,128)S(1)} %copy-done.7, f32[5,2,96,1361]{3,2,1,0:T(8,128)S(1)} %fusion.1, f32[5,2,96,1361]{3,2,1,0:T(8,128)} %broadcast_select_fusion), kind=kLoop, calls=%fused_computation.27 | loop fusion | flops 9145920 | bytes 23518080 | tf_op jit(solution)/shard_map/add | solution.py:113
  101.4 6.5 %dynamic_update_slice.15 = f32[2,96,2081]{2,1,0:T(8,128)} dynamic-update-slice(f32[2,96,2081]{2,1,0:T(8,128)} %broadcast_in_dim.142, f32[2,96,1361]{2,1,0:T(8,128)} %fusion.22, s32[]{:T(128)} %constant.31.clone.1, s32[]{:T(128)} %constant.31.clone.1, s32[]{:T(128)S(6)} %select_n.152) | dynamic-update-slice | bytes 2090500 | tf_op jit(solution)/shard_map/dynamic_update_slice | solution.py:119
  107.9 2.8 %fusion.26 = f32[2,96,1361]{2,1,0:T(8,128)} fusion(f32[5,1,96,1361]{3,2,1,0:T(8,128)S(1)} %get-tuple-element.17, f32[5,1,96,1361]{3,2,1,0:T(8,128)} %copy-done.1, f32[2,96,2081]{2,1,0:T(8,128)} %dynamic_update_slice.15, s32[]{:T(128)S(6)} %select_n.153, pred[1361]{0:T(1024)(128)(4,1)S(1)} %get-tuple-element.10), kind=kLoop, calls=%fused_computation.60 | loop fusion | flops 783936 | bytes 7318101 | tf_op jit(solution)/shard_map/add | solution.py:119
  110.7 6.5 %dynamic_update_slice.16 = f32[2,96,2081]{2,1,0:T(8,128)} dynamic-update-slice(f32[2,96,2081]{2,1,0:T(8,128)} %dynamic_update_slice.15, f32[2,96,1361]{2,1,0:T(8,128)} %fusion.26, s32[]{:T(128)} %constant.31.clone.1, s32[]{:T(128)} %constant.31.clone.1, s32[]{:T(128)S(6)} %select_n.153) | dynamic-update-slice | bytes 2090500 | tf_op jit(solution)/shard_map/dynamic_update_slice | solution.py:119
  117.2 2.8 %fusion.30 = f32[2,96,1361]{2,1,0:T(8,128)} fusion(f32[5,1,96,1361]{3,2,1,0:T(8,128)S(1)} %get-tuple-element.17, f32[5,1,96,1361]{3,2,1,0:T(8,128)} %copy-done.1, f32[2,96,2081]{2,1,0:T(8,128)} %dynamic_update_slice.16, s32[]{:T(128)S(6)} %select_n.154, pred[1361]{0:T(1024)(128)(4,1)S(1)} %get-tuple-element.9), kind=kLoop, calls=%fused_computation.64 | loop fusion | flops 783936 | bytes 7318101 | tf_op jit(solution)/shard_map/add | solution.py:119
  120.0 6.5 %dynamic_update_slice.17 = f32[2,96,2081]{2,1,0:T(8,128)} dynamic-update-slice(f32[2,96,2081]{2,1,0:T(8,128)} %dynamic_update_slice.16, f32[2,96,1361]{2,1,0:T(8,128)} %fusion.30, s32[]{:T(128)} %constant.31.clone.1, s32[]{:T(128)} %constant.31.clone.1, s32[]{:T(128)S(6)} %select_n.154) | dynamic-update-slice | bytes 2090500 | tf_op jit(solution)/shard_map/dynamic_update_slice | solution.py:119
  128.6 10.7 %multiply_convert_fusion = (bf16[5,2,2,2,96,1361]{5,4,1,3,2,0:T(8,128)(2,1)}, bf16[5,2,2,2,96,1361]{5,4,1,3,2,0:T(8,128)(2,1)}) fusion(f32[5,2,96,1361]{3,2,1,0:T(8,128)} %maximum_convert_fusion.1, f32[5,2,2,1361]{3,1,2,0:T(2,128)S(1)} %and_convert_fusion, f32[5,2,96,1361]{3,2,1,0:T(8,128)S(1)} %maximum_convert_fusion), kind=kLoop, calls=%fused_computation.5 | loop fusion | flops 20904960 | bytes 31466320 | tf_op jit(solution)/shard_map/convert_element_type | solution.py:128
  139.3 6.4 %fusion.2 = f32[5,2,2,2,96,8]{4,5,3,2,1,0:T(8,128)S(1)} fusion(bf16[5,2,2,2,96,1361]{5,4,1,3,2,0:T(8,128)(2,1)} %get-tuple-element.49, bf16[5,1361,8]{1,2,0:T(8,128)(2,1)S(1)} %copy-done), kind=kOutput, calls=%fused_computation.7 | convolution fusion | flops 83619840 | bytes 10684240 | tf_op jit(solution)/shard_map/pqk,phercq->kecrph/dot_general | solution.py:129
  147.1 6.5 %dynamic_update_slice.18 = f32[2,96,2081]{2,1,0:T(8,128)} dynamic-update-slice(f32[2,96,2081]{2,1,0:T(8,128)} %dynamic_update_slice.17, f32[2,96,1361]{2,1,0:T(8,128)} %fusion.34, s32[]{:T(128)} %constant.31.clone.1, s32[]{:T(128)} %constant.31.clone.1, s32[]{:T(128)S(6)} %select_n.155) | dynamic-update-slice | bytes 2090500 | tf_op jit(solution)/shard_map/dynamic_update_slice | solution.py:119
  154.5 3.6 %all-to-all-start.2 = ((bf16[8,2,96,2,10]{2,3,4,1,0:T(2,128)(2,1)}), bf16[8,2,96,2,10]{2,3,4,1,0:T(2,128)(2,1)S(1)}, u32[]{:S(2)}, u32[]{:S(2)}) async-start(bf16[8,2,96,2,10]{2,3,4,1,0:T(2,128)(2,1)} %pad_maximum_fusion.4), calls=%async_computation.2 | async-start | bytes 163840 | tf_op jit(solution)/shard_map/all_to_all | solution.py:136
  158.1 6.4 %fusion.4 = f32[5,2,2,2,96,8]{4,5,3,2,1,0:T(8,128)S(1)} fusion(bf16[5,2,2,2,96,1361]{5,4,1,3,2,0:T(8,128)(2,1)} %get-tuple-element.50, bf16[5,1361,8]{1,2,0:T(8,128)(2,1)S(1)} %copy-done), kind=kOutput, calls=%fused_computation.9 | convolution fusion | flops 83619840 | bytes 10684240 | tf_op jit(solution)/shard_map/pqk,phercq->kecrph/dot_general | solution.py:129
  168.3 6.5 %dynamic_update_slice.19 = f32[2,96,2081]{2,1,0:T(8,128)} dynamic-update-slice(f32[2,96,2081]{2,1,0:T(8,128)} %dynamic_update_slice.18, f32[2,96,1361]{2,1,0:T(8,128)} %fusion.38, s32[]{:T(128)} %constant.31.clone.1, s32[]{:T(128)} %constant.31.clone.1, s32[]{:T(128)S(6)} %select_n.156) | dynamic-update-slice | bytes 2090500 | tf_op jit(solution)/shard_map/dynamic_update_slice | solution.py:119
  174.8 3.9 %all-to-all-start.1 = ((bf16[8,2,96,2,10]{2,3,4,1,0:T(2,128)(2,1)}), bf16[8,2,96,2,10]{2,3,4,1,0:T(2,128)(2,1)S(1)}, u32[]{:S(2)}, u32[]{:S(2)}) async-start(bf16[8,2,96,2,10]{2,3,4,1,0:T(2,128)(2,1)} %pad_maximum_fusion.3), calls=%async_computation.1 | async-start | bytes 163840 | tf_op jit(solution)/shard_map/all_to_all | solution.py:135
  180.9 2.9 %all-to-all-done.1 = bf16[8,2,96,2,10]{2,3,4,1,0:T(2,128)(2,1)S(1)} async-done(((bf16[8,2,96,2,10]{2,3,4,1,0:T(2,128)(2,1)}), bf16[8,2,96,2,10]{2,3,4,1,0:T(2,128)(2,1)S(1)}, u32[]{:S(2)}, u32[]{:S(2)}) %all-to-all-start.1) | async-done | bytes 61472 | tf_op jit(solution)/shard_map/all_to_all | solution.py:135
  184.1 6.1 %copy.78 = bf16[1,2,384,1440]{2,3,1,0:T(8,128)(2,1)S(1)} copy(bf16[1,2,384,1440]{3,1,0,2:T(2,128)(2,1)} %all-gather.3.cloned.1.call-done) | data formatting | bytes 4423680 | tf_op jit(solution)/shard_map/all_gather | solution.py:146
  191.4 6.8 %copy.90 = bf16[1,2,384,1440]{2,3,1,0:T(8,128)(2,1)} copy(bf16[1,2,384,1440]{3,1,0,2:T(2,128)(2,1)} %all-gather.5.cloned.1.call-done) | data formatting | bytes 4423680 | tf_op jit(solution)/shard_map/all_gather | solution.py:147
  204.1 40.8 %all-reduce.5.cloned.1.call-done = (f32[96,2,720]{2,0,1:T(8,128)}, f32[384,96]{0,1:T(8,128)}) async-done(((f32[96,2,720]{2,0,1:T(8,128)}, f32[384,96]{0,1:T(8,128)}), (f32[96,2,720]{2,0,1:T(8,128)}, f32[384,96]{0,1:T(8,128)})) %all-reduce.5.cloned.1.call-update) | async-done | bytes 700432 | tf_op jit(solution)/shard_map/psum | solution.py:162
  (136 shorter events, 60.3 us)
Async XLA Ops:
  7.2 73.8 %copy-start = (bf16[5,1361,8]{1,2,0:T(8,128)(2,1)S(1)}, bf16[5,1361,8]{1,2,0:T(8,128)(2,1)}, u32[]{:S(2)}) copy-start(bf16[5,1361,8]{1,2,0:T(8,128)(2,1)} %param.8) | copy-start | bytes 326644
  7.2 13.8 %copy-start.16 = (bf16[1,2,96,1440]{3,2,1,0:T(8,128)(2,1)S(1)}, bf16[1,2,96,1440]{3,2,1,0:T(8,128)(2,1)}, u32[]{:S(2)}) copy-start(bf16[1,2,96,1440]{3,2,1,0:T(8,128)(2,1)} %param.6) | copy-start | bytes 1658884
  7.2 176.9 %all-gather.3.cloned.1.call-start = ((), (), s32[]{:S(2)}) async-start(), calls=%async_computation.3 | async-start | bytes 2949120 | tf_op jit(solution)/shard_map/all_gather | solution.py:146
  9.8 16.4 %copy-start.12 = (bf16[1,2,96,1440]{3,2,1,0:T(8,128)(2,1)S(1)}, bf16[1,2,96,1440]{3,2,1,0:T(8,128)(2,1)}, u32[]{:S(2)}) copy-start(bf16[1,2,96,1440]{3,2,1,0:T(8,128)(2,1)} %param.7) | copy-start | bytes 1658884
  13.7 13.9 %copy-start.14 = (bf16[1440,1,80]{0,2,1:T(8,128)(2,1)}, bf16[1440,1,80]{0,2,1:T(8,128)(2,1)S(1)}, u32[]{:S(2)}) copy-start(bf16[1440,1,80]{0,2,1:T(8,128)(2,1)S(1)} %get-tuple-element.59) | copy-start | bytes 691204
  13.7 13.9 %copy-start.18 = (s32[40]{0:T(128)S(1)}, s32[40]{0:T(128)}, u32[]{:S(2)}) copy-start(s32[40]{0:T(128)} %param.11) | copy-start | bytes 484
  13.7 21.2 %copy-start.10 = (f32[96,2,720]{2,1,0:T(2,128)S(1)}, f32[96,2,720]{2,1,0:T(2,128)}, u32[]{:S(2)}) copy-start(f32[96,2,720]{2,1,0:T(2,128)} %param.9) | copy-start | bytes 1658884
  16.2 56.9 %collective-permute-start = (bf16[1,2,96,2,10]{2,3,4,1,0:T(2,128)(2,1)}, bf16[1,2,96,2,10]{2,3,4,1,0:T(2,128)(2,1)}, u32[]{:S(2)}, u32[]{:S(2)}) collective-permute-start(bf16[1,2,96,2,10]{2,3,4,1,0:T(2,128)(2,1)} %get-tuple-element.40), channel_id=1, source_target_pairs={{0,4},{4,0},{8,12},{12,8},{16,20},{20,16},{24,28},{28,24},{1,5},{5... | collective-permute-start | bytes 23048 | tf_op jit(solution)/shard_map/ppermute | solution.py:25
  16.6 59.5 %collective-permute-start.1 = (bf16[1,2,96,2,10]{2,3,4,1,0:T(2,128)(2,1)}, bf16[1,2,96,2,10]{2,3,4,1,0:T(2,128)(2,1)}, u32[]{:S(2)}, u32[]{:S(2)}) collective-permute-start(bf16[1,2,96,2,10]{2,3,4,1,0:T(2,128)(2,1)} %get-tuple-element.39), channel_id=1, source_target_pairs={{0,8},{4,12},{8,0},{12,4},{16,24},{20,28},{24,16},{28,20},{1,9},{5... | collective-permute-start | bytes 23048 | tf_op jit(solution)/shard_map/ppermute | solution.py:25
  19.1 57.9 %collective-permute-start.2 = (bf16[1,2,96,2,10]{2,3,4,1,0:T(2,128)(2,1)S(1)}, bf16[1,2,96,2,10]{2,3,4,1,0:T(2,128)(2,1)}, u32[]{:S(2)}, u32[]{:S(2)}) collective-permute-start(bf16[1,2,96,2,10]{2,3,4,1,0:T(2,128)(2,1)S(1)} %get-tuple-element.38), channel_id=1, source_target_pairs={{0,12},{4,8},{8,4},{12,0},{16,28},{20,24},{24,20},{28,16},{1,13},{... | collective-permute-start | bytes 23048 | tf_op jit(solution)/shard_map/ppermute | solution.py:25
  19.3 58.4 %collective-permute-start.3 = (bf16[1,2,96,2,10]{2,3,4,1,0:T(2,128)(2,1)S(1)}, bf16[1,2,96,2,10]{2,3,4,1,0:T(2,128)(2,1)}, u32[]{:S(2)}, u32[]{:S(2)}) collective-permute-start(bf16[1,2,96,2,10]{2,3,4,1,0:T(2,128)(2,1)S(1)} %get-tuple-element.37), channel_id=1, source_target_pairs={{0,16},{4,20},{8,24},{12,28},{16,0},{20,4},{24,8},{28,12},{1,17},{... | collective-permute-start | bytes 23048 | tf_op jit(solution)/shard_map/ppermute | solution.py:25
  21.0 57.4 %collective-permute-start.4 = (bf16[1,2,96,2,10]{2,3,4,1,0:T(2,128)(2,1)S(1)}, bf16[1,2,96,2,10]{2,3,4,1,0:T(2,128)(2,1)}, u32[]{:S(2)}, u32[]{:S(2)}) collective-permute-start(bf16[1,2,96,2,10]{2,3,4,1,0:T(2,128)(2,1)S(1)} %get-tuple-element.36), channel_id=1, source_target_pairs={{0,20},{4,16},{8,28},{12,24},{16,4},{20,0},{24,12},{28,8},{1,21},{... | collective-permute-start | bytes 23048 | tf_op jit(solution)/shard_map/ppermute | solution.py:25
  22.2 67.8 %all-to-all-start = ((bf16[1,2,96,2,80]{2,1,3,0,4:T(2,128)(2,1)}), bf16[1,2,96,2,80]{2,1,3,0,4:T(2,128)(2,1)S(1)}, u32[]{:S(2)}, u32[]{:S(2)}) async-start(bf16[1,2,96,2,80]{2,1,3,0,4:T(2,128)(2,1)} %copy.68), calls=%async_computation | async-start | bytes 163840 | tf_op jit(solution)/shard_map/all_to_all | solution.py:63
  26.1 165.3 %all-gather.5.cloned.1.call-start = ((), (), s32[]{:S(2)}) async-start(), calls=%async_computation.4 | async-start | bytes 2949120 | tf_op jit(solution)/shard_map/all_gather | solution.py:147
  73.1 6.1 %collective-permute-start.5 = (bf16[1,2,96,2,10]{2,3,4,1,0:T(2,128)(2,1)S(1)}, bf16[1,2,96,2,10]{2,3,4,1,0:T(2,128)(2,1)S(1)}, u32[]{:S(2)}, u32[]{:S(2)}) collective-permute-start(bf16[1,2,96,2,10]{2,3,4,1,0:T(2,128)(2,1)S(1)} %get-tuple-element.35), channel_id=1, source_target_pairs={{0,24},{4,28},{8,16},{12,20},{16,8},{20,12},{24,0},{28,4},{1,25},{... | collective-permute-start | bytes 23048 | tf_op jit(solution)/shard_map/ppermute | solution.py:25
  76.2 4.1 %collective-permute-start.6 = (bf16[1,2,96,2,10]{2,3,4,1,0:T(2,128)(2,1)S(1)}, bf16[1,2,96,2,10]{2,3,4,1,0:T(2,128)(2,1)S(1)}, u32[]{:S(2)}, u32[]{:S(2)}) collective-permute-start(bf16[1,2,96,2,10]{2,3,4,1,0:T(2,128)(2,1)S(1)} %get-tuple-element.34), channel_id=1, source_target_pairs={{0,28},{4,24},{8,20},{12,16},{16,12},{20,8},{24,4},{28,0},{1,29},{... | collective-permute-start | bytes 23048 | tf_op jit(solution)/shard_map/ppermute | solution.py:25
  139.3 6.4 %copy-start.2 = (f32[5,1,96,1361]{3,2,1,0:T(8,128)S(1)}, f32[5,1,96,1361]{3,2,1,0:T(8,128)}, u32[]{:S(2)}) copy-start(f32[5,1,96,1361]{3,2,1,0:T(8,128)} %copy-done.1) | copy-start | bytes 7839364
  139.3 6.4 %copy-start.4 = (f32[2,96,2081]{2,1,0:T(8,128)S(1)}, f32[2,96,2081]{2,1,0:T(8,128)}, u32[]{:S(2)}) copy-start(f32[2,96,2081]{2,1,0:T(8,128)} %dynamic_update_slice.17) | copy-start | bytes 4794628
  154.5 20.3 %all-to-all-start.2 = ((bf16[8,2,96,2,10]{2,3,4,1,0:T(2,128)(2,1)}), bf16[8,2,96,2,10]{2,3,4,1,0:T(2,128)(2,1)S(1)}, u32[]{:S(2)}, u32[]{:S(2)}) async-start(bf16[8,2,96,2,10]{2,3,4,1,0:T(2,128)(2,1)} %pad_maximum_fusion.4), calls=%async_computation.2 | async-start | bytes 163840 | tf_op jit(solution)/shard_map/all_to_all | solution.py:136
  158.1 6.6 %copy-start.3 = (f32[5,1,96,1361]{3,2,1,0:T(8,128)S(1)}, f32[5,1,96,1361]{3,2,1,0:T(8,128)}, u32[]{:S(2)}) copy-start(f32[5,1,96,1361]{3,2,1,0:T(8,128)} %copy-done.1) | copy-start | bytes 7839364
  167.5 11.2 %copy-start.9 = (f32[2,96,1361]{2,1,0:T(8,128)S(1)}, f32[2,96,1361]{2,1,0:T(8,128)}, u32[]{:S(2)}) copy-start(f32[2,96,1361]{2,1,0:T(8,128)} %fusion.7) | copy-start | bytes 3135748
  174.8 9.0 %all-to-all-start.1 = ((bf16[8,2,96,2,10]{2,3,4,1,0:T(2,128)(2,1)}), bf16[8,2,96,2,10]{2,3,4,1,0:T(2,128)(2,1)S(1)}, u32[]{:S(2)}, u32[]{:S(2)}) async-start(bf16[8,2,96,2,10]{2,3,4,1,0:T(2,128)(2,1)} %pad_maximum_fusion.3), calls=%async_computation.1 | async-start | bytes 163840 | tf_op jit(solution)/shard_map/all_to_all | solution.py:135
  178.7 66.2 %all-reduce.5.cloned.1.call-start = ((), (), s32[]{:S(2)}) async-start(), calls=%async_computation.5 | async-start | bytes 1474560 | tf_op jit(solution)/shard_map/psum | solution.py:162
  180.9 9.3 %copy-start.13 = (bf16[1,2,96,1440]{3,2,1,0:T(8,128)(2,1)S(1)}, bf16[1,2,96,1440]{3,2,1,0:T(8,128)(2,1)}, u32[]{:S(2)}) copy-start(bf16[1,2,96,1440]{3,2,1,0:T(8,128)(2,1)} %param.7) | copy-start | bytes 1658884
  (10 other events, 30.8 us)
Sparse Core Ops, SparseCore 0:
  10.2 53.8 all-gather.2
  66.2 49.4 all-gather.4
  191.5 53.2 all-reduce.4
